TPU v7x, 32 devices: a whole 2x2x4 slice. The times are simulated.
32 devices in a mesh: strip: 8 (over y, x, core), lag: 4 (over z).
Axes of the slice: x: 2, y: 2, z: 4, core: 2. Of those that a mesh axis runs over, the one named last changes fastest.
Arguments:
- image_grad: float32 [128, 512, 1024], P('lag', 'strip'), may hold values from -0.4 to 0.4
- source_field: float32 [2, 512, 1024], P(None, None, 'strip'), may hold values from -6 to 6
- receiver_field: float32 [2, 512, 1024], P(None, None, 'strip'), may hold values from -6 to 6
Outputs:
- source_adjoint: float32 [2, 512, 1024], P(None, 'strip', 'lag')
- receiver_adjoint: float32 [2, 512, 1024], P(None, 'strip', 'lag')
All inputs are finite; a program needn't handle non-finite values.
Results may differ from a plain program's by a relative error of at most 0.0003.
Values sent between devices are 32-bit elements; how exact they have to be, the bound alone decides.
No kernel may reach another device: no remote copies, remote signals or barrier semaphores. Data moves between devices by JAX's collectives and lax.ppermute only.
A program may use at most 128 MiB of HBM per device.

v0:
```python
import functools

import jax
import jax.numpy as jnp
from jax import lax
from jax.experimental import pallas as pl
from jax.experimental.pallas import tpu as pltpu
from jax.sharding import PartitionSpec as P

LANES = 128
ROWS = 8
CLASSES = 4
PAIRS = 4
FILTER_BYTES = 24 * 1024 * 1024
SUM_BYTES = 8 * 1024 * 1024
SMALL_BYTES = 4 * 1024 * 1024

whole_vmem = pl.BlockSpec(memory_space=pltpu.VMEM)


def chain_halo(rows, axis, step):
    count = lax.axis_size(axis)
    pairs = [(i, i + step) for i in range(count) if 0 <= i + step < count]
    return lax.ppermute(rows, axis, pairs)


def filter_kernel(pad, grad_hbm, above_ref, below_ref, out_ref, *turned):
    lag_count, depth, width = grad_hbm.shape
    half = lag_count // 2
    tiles = width // LANES
    centers, uprights = turned[:PAIRS], turned[PAIRS:]
    out_ref[:, pl.ds(0, pad)] = jnp.zeros((half, pad, LANES), jnp.float32)
    out_ref[:, pl.ds(pad + width, pad)] = jnp.zeros((half, pad, LANES), jnp.float32)
    for center_t in centers:
        center_t[pl.ds(0, ROWS)] = jnp.zeros((ROWS, LANES), jnp.float32)
        center_t[pl.ds(ROWS + width, ROWS)] = jnp.zeros((ROWS, LANES), jnp.float32)

    def body(low_ref, high_ref):
        step = pl.program_id(0)
        row = lax.broadcasted_iota(jnp.int32, (depth, LANES), 0)

        def turn(within, t):
            lanes = pl.ds(t * LANES, LANES)
            mids, stencils = [], []
            for slab, shift in ((low_ref, 0), (high_ref, half)):
                lag = step * PAIRS + within + shift
                mid = slab[within, :, lanes]
                up = jnp.where(row == 0, above_ref[lag, :, lanes], pltpu.roll(mid, 1, 0))
                down = jnp.where(row == depth - 1, below_ref[lag, :, lanes], pltpu.roll(mid, depth - 1, 0))
                mids.append(mid)
                stencils.append(2.0 * mid - 0.25 * (up + down))
            centers[within][pl.ds(ROWS + t * LANES, LANES)] = jnp.concatenate(mids, 0).T
            uprights[within][pl.ds(t * LANES, LANES)] = jnp.concatenate(stencils, 0).T

        def join(within, t):
            west = centers[within][pl.ds(ROWS - 1 + t * LANES, LANES)]
            east = centers[within][pl.ds(ROWS + 1 + t * LANES, LANES)]
            upright = uprights[within][pl.ds(t * LANES, LANES)]
            out_ref[step * PAIRS + within, pl.ds(pad + t * LANES, LANES)] = upright - 0.25 * (west + east)

        for within in range(PAIRS + 1):
            for t in range(tiles):
                if within < PAIRS:
                    turn(within, t)
                if within:
                    join(within - 1, t)

    pltpu.emit_pipeline(
        body,
        grid=(half // PAIRS,),
        in_specs=[
            pl.BlockSpec((PAIRS, depth, width), lambda i: (i, 0, 0)),
            pl.BlockSpec((PAIRS, depth, width), lambda i: (i + half // PAIRS, 0, 0)),
        ],
        out_specs=[],
    )(grad_hbm, grad_hbm)


def filter_slabs(image_grad, above, below, pad):
    lag_count, depth, width = image_grad.shape
    return pl.pallas_call(
        functools.partial(filter_kernel, pad),
        out_shape=jax.ShapeDtypeStruct((lag_count // 2, width + 2 * pad, 2 * depth), jnp.float32),
        in_specs=[pl.BlockSpec(memory_space=pltpu.HBM), whole_vmem, whole_vmem],
        out_specs=whole_vmem,
        scratch_shapes=[pltpu.VMEM((width + 2 * ROWS, LANES), jnp.float32)] * PAIRS
        + [pltpu.VMEM((width, LANES), jnp.float32)] * PAIRS,
        compiler_params=pltpu.CompilerParams(vmem_limit_bytes=FILTER_BYTES),
        cost_estimate=pl.CostEstimate(
            flops=8 * lag_count * depth * width, bytes_accessed=8 * lag_count * depth * width, transcendentals=0
        ),
        name="filter_slabs",
    )(image_grad, above, below)


def sum_kernel(sign, places, where_at, slab_ref, *refs):
    pieces, (keep_ref, send_ref, field_ref, paired, acc) = refs[:-5], refs[-5:]
    half, slab_rows, _ = slab_ref.shape
    width = field_ref.shape[0]
    if where_at is None:
        field_ref[...] = pieces[0][...]
    else:
        columns = pieces[0].shape[-2]
        strip = lax.axis_index("strip")
        for index, block, distance in where_at:
            rows = pl.multiple_of((strip ^ distance) * columns, columns)
            field_ref[pl.ds(rows, columns)] = pieces[index][block]
    pad = (slab_rows - width) // 2
    lag_count = 2 * half
    margin = 2 * pad + 2 * half
    place = lax.axis_index("lag")
    first = place * lag_count - pad
    spread = width + half
    block_rows = ROWS * max(m for m in range(1, 11) if spread // ROWS % m == 0)
    low_at = 0 if sign > 0 else half
    high_at = half - low_at

    for snap in range(2):
        blank = jnp.zeros((margin + half, LANES), jnp.float32)
        paired[snap, pl.ds(0, margin)] = blank[:margin]
        paired[snap, pl.ds(margin + width, margin)] = blank[:margin]
    low = lax.broadcasted_iota(jnp.int32, (LANES, LANES), 1) < LANES // 2
    edge = jnp.zeros((half, LANES), jnp.float32)
    field = field_ref[...]
    lower = lax.broadcasted_iota(jnp.int32, (spread, LANES), 1) < LANES // 2
    if sign > 0:
        here = jnp.concatenate([edge, field], 0)
        there = jnp.concatenate([field, edge], 0)
        start = margin - half
    else:
        here = jnp.concatenate([field, edge], 0)
        there = jnp.concatenate([edge, field], 0)
        start = margin
    paired[0, pl.ds(start, spread)] = jnp.where(lower, here, pltpu.roll(there, LANES // 2, 1))
    paired[1, pl.ds(start, spread)] = jnp.where(lower, pltpu.roll(here, LANES // 2, 1), there)

    tall = block_rows // ROWS
    per_class = half // CLASSES

    def block(at, carry):
        y = at * block_rows - low_at
        slab_at = pl.multiple_of(pad + y + sign * first, ROWS)
        field_at = pl.multiple_of(margin + y + sign * 2 * first, ROWS)
        totals = [[None] * tall for _ in range(2)]
        for cls in range(CLASSES):
            held = {}
            for step in range(per_class):
                lag = step * CLASSES + cls
                for up in range(tall):
                    slab = slab_ref[lag, pl.ds(slab_at + sign * lag + up * ROWS, ROWS)]
                    for snap in range(2):
                        row = sign * 2 * lag + up * ROWS
                        if (snap, row) not in held:
                            held[snap, row] = paired[snap, pl.ds(field_at + row, ROWS)]
                        term = slab * held[snap, row]
                        total = totals[snap][up]
                        totals[snap][up] = term if total is None else total + term
        for snap in range(2):
            for up in range(tall):
                rows = pl.multiple_of(at * block_rows + up * ROWS, ROWS)
                acc[snap, pl.ds(rows, ROWS)] = totals[snap][up]
        return carry

    lax.fori_loop(0, spread // block_rows, block, 0)

    part = width // places

    def finish(target, slot, source):
        for piece in range(part // LANES):
            x = pl.multiple_of(source * part + piece * LANES, LANES)
            at_low = pl.ds(x + low_at, LANES)
            at_high = pl.ds(x + high_at, LANES)
            straight = jnp.where(low, acc[0, at_low], acc[1, at_high])
            crossed = jnp.where(low, acc[1, at_low], acc[0, at_high])
            target[slot, pl.ds(piece * LANES, LANES)] = straight + pltpu.roll(crossed, LANES // 2, 1)

    other = place + 1 - 2 * lax.rem(place, 2)
    finish(send_ref, 0, other)
    finish(send_ref, 1, places - 1 - other)
    finish(keep_ref, 0, place)
    finish(keep_ref, 1, places - 1 - place)


def sum_lags(sign, slabs, pieces, where_at, width):
    half, slab_rows, _ = slabs.shape
    pad = (slab_rows - width) // 2
    margin = 2 * pad + 2 * half
    places = lax.axis_size("lag")
    part = jax.ShapeDtypeStruct((2, width // places, LANES), jnp.float32)
    return pl.pallas_call(
        functools.partial(sum_kernel, sign, places, where_at),
        out_shape=[part, part],
        in_specs=[whole_vmem] * (1 + len(pieces)),
        out_specs=[whole_vmem] * 2,
        scratch_shapes=[
            pltpu.VMEM((width, LANES), jnp.float32),
            pltpu.VMEM((2, width + 2 * margin, LANES), jnp.float32),
            pltpu.VMEM((2, width + half, LANES), jnp.float32),
        ],
        compiler_params=pltpu.CompilerParams(vmem_limit_bytes=SUM_BYTES),
        cost_estimate=pl.CostEstimate(
            flops=8 * half * width * LANES, bytes_accessed=4 * half * slab_rows * LANES, transcendentals=0
        ),
        name="sum_lags",
    )(slabs, *pieces)


def cut_kernel(*refs):
    half = len(refs) // 3
    strip = lax.axis_index("strip")
    for index, field_ref in enumerate(refs[:half]):
        near_ref, far_ref = refs[half + 2 * index : half + 2 * index + 2]
        snaps = field_ref.shape[0]
        count, _, lanes = near_ref.shape
        depth = lanes // snaps
        for at in range(count):
            for out_ref, side in ((far_ref, 1), (near_ref, 0)):
                first = pl.multiple_of((strip ^ (2 * at + side)) * depth, depth)
                rows = [field_ref[s, pl.ds(first, depth)] for s in range(snaps)]
                out_ref[at] = jnp.concatenate(rows, 0).T


def pack_kernel(fields, *refs):
    near, far, out = refs[:fields], refs[fields : 2 * fields], refs[2 * fields :]
    distances = len(out) // fields
    for f in range(fields):
        for at in range(distances):
            out[f * distances + at][0] = near[f][at + 1]
            out[f * distances + at][1] = far[f][at + 1]


def fields_by_rows(fields):
    count = lax.axis_size("strip")
    snaps, all_rows, columns = fields[0].shape
    depth = all_rows // count
    if columns != LANES or count & (count - 1) or count < 4:
        whole = []
        for field in fields:
            cut = field.reshape(snaps, count, depth, columns).transpose(1, 3, 0, 2)
            cut = lax.all_to_all(cut.reshape(count, columns, snaps * depth), "strip", 0, 0, tiled=True)
            whole.append([cut.reshape(count * columns, snaps * depth)])
        return whole, None
    number = len(fields)
    cut = jax.ShapeDtypeStruct((count // 2, columns, snaps * depth), jnp.float32)
    parts = pl.pallas_call(
        cut_kernel,
        out_shape=[cut] * (2 * number),
        in_specs=[whole_vmem] * number,
        out_specs=[whole_vmem] * (2 * number),
        compiler_params=pltpu.CompilerParams(vmem_limit_bytes=SMALL_BYTES),
        name="cut_fields",
    )(*fields)

    def swap(part, distance):
        return lax.ppermute(part, "strip", [(i, i ^ distance) for i in range(count)])

    near, far = parts[0::2], [swap(part, 1) for part in parts[1::2]]
    distances = count // 2 - 1
    pair = jax.ShapeDtypeStruct((2, columns, snaps * depth), jnp.float32)
    packed = pl.pallas_call(
        functools.partial(pack_kernel, number),
        out_shape=[pair] * (distances * number),
        in_specs=[whole_vmem] * (2 * number),
        out_specs=[whole_vmem] * (distances * number),
        compiler_params=pltpu.CompilerParams(vmem_limit_bytes=SMALL_BYTES),
        name="pack_fields",
    )(*near, *far)
    where_at = [(0, 0, 0), (1, 0, 1)]
    where_at += [(2 + at, side, 2 * at + 2 + side) for at in range(distances) for side in range(2)]
    whole = []
    for f in range(number):
        sent = [swap(packed[f * distances + at], 2 * at + 2) for at in range(distances)]
        whole.append([near[f], far[f], *sent])
    return whole, where_at


def exchange(parts, distance):
    count = lax.axis_size("lag")
    return lax.ppermute(parts, "lag", [(i, i ^ distance) for i in range(count)])


def turn_back_kernel(first_ref, second_ref, out_ref):
    snaps, depth, _ = out_ref.shape
    for at in range(first_ref.shape[0] // LANES):
        rows = pl.ds(at * LANES, LANES)
        turned = (first_ref[rows] + second_ref[rows]).T
        for snap in range(snaps):
            out_ref[snap, :, rows] = turned[snap * depth : (snap + 1) * depth]


def sum_places(keep, send, snaps):
    both = keep + exchange(send, 1)
    rows, lanes = both.shape[1:]
    return pl.pallas_call(
        turn_back_kernel,
        out_shape=jax.ShapeDtypeStruct((snaps, lanes // snaps, rows), jnp.float32),
        in_specs=[whole_vmem] * 2,
        out_specs=whole_vmem,
        compiler_params=pltpu.CompilerParams(vmem_limit_bytes=SMALL_BYTES),
        name="turn_back",
    )(both[0], exchange(both[1], 3))


def local(image_grad, source_field, receiver_field):
    lag_count, depth, width = image_grad.shape
    snaps = source_field.shape[0]
    pad = lax.axis_size("lag") * lag_count // 2
    (receiver, source), where_at = fields_by_rows([receiver_field, source_field])
    above = chain_halo(image_grad[:, depth - 1 :], "strip", 1)
    below = chain_halo(image_grad[:, :1], "strip", -1)
    slabs = filter_slabs(image_grad, above, below, pad)
    source_adjoint = sum_places(*sum_lags(1, slabs, receiver, where_at, width), snaps)
    receiver_adjoint = sum_places(*sum_lags(-1, slabs, source, where_at, width), snaps)
    return source_adjoint, receiver_adjoint


def solution(mesh):
    in_specs = (P("lag", "strip", None), P(None, None, "strip"), P(None, None, "strip"))
    out_specs = (P(None, "strip", "lag"), P(None, "strip", "lag"))
    return jax.shard_map(local, mesh=mesh, in_specs=in_specs, out_specs=out_specs, check_vma=False)
```

profile of v0, /device:TPU:0, one launch (start us, length us, event | category | flops | bytes accessed | tf_op | source)
XLA Modules:
  0.0 58.4 jit_solution(14343197907902906406)
XLA Ops:
  0.6 0.0 copy-start.1
  0.6 1.0 %copy-done.1 = f32[2,512,128]{2,1,0:T(8,128)S(1)} copy-done((f32[2,512,128]{2,1,0:T(8,128)S(1)}, f32[2,512,128]{2,1,0:T(8,128)}, u32[]{:S(2)}) %copy-start.1) | copy-done | bytes 524312
  1.7 0.0 copy-start.2
  1.7 1.0 %copy-done.2 = f32[2,512,128]{2,1,0:T(8,128)S(1)} copy-done((f32[2,512,128]{2,1,0:T(8,128)S(1)}, f32[2,512,128]{2,1,0:T(8,128)}, u32[]{:S(2)}) %copy-start.2) | copy-done | bytes 524312
  2.7 0.3 cut_fields.1
  3.1 0.5 collective-permute-start.2
  3.6 0.1 collective-permute-start.3
  3.6 1.8 %fusion = (f32[32,1,1024]{2,1,0:T(1,128)S(1)}, f32[32,1,1024]{2,1,0:T(1,128)S(1)}) fusion(f32[32,64,1024]{2,1,0:T(8,128)} %grad_hbm.1), kind=kLoop, calls=%fused_computation.4 | loop fusion | bytes 524288 | tf_op jit(solution)/shard_map/slice | solution.py:310
  5.4 1.3 %collective-permute-start.1 = (f32[32,1,1024]{2,1,0:T(1,128)S(1)}, f32[32,1,1024]{2,1,0:T(1,128)S(1)}, u32[]{:S(2)}, u32[]{:S(2)}) collective-permute-start(f32[32,1,1024]{2,1,0:T(1,128)S(1)} %get-tuple-element.30), channel_id=1, source_target_pairs={{4,0},{8,4},{12,8},{16,12},{20,16},{24,20},{28,24},{5,1},{9,5},{13... | collective-permute-start | bytes 393224 | tf_op jit(solution)/shard_map/ppermute | solution.py:24
  6.7 3.0 %collective-permute-start = (f32[32,1,1024]{2,1,0:T(1,128)S(1)}, f32[32,1,1024]{2,1,0:T(1,128)S(1)}, u32[]{:S(2)}, u32[]{:S(2)}) collective-permute-start(f32[32,1,1024]{2,1,0:T(1,128)S(1)} %get-tuple-element.31), channel_id=1, source_target_pairs={{0,4},{4,8},{8,12},{12,16},{16,20},{20,24},{24,28},{1,5},{5,9},{9,... | collective-permute-start | bytes 393224 | tf_op jit(solution)/shard_map/ppermute | solution.py:24
  9.8 0.0 collective-permute-done.2.refs_2_.refs_1_
  9.8 0.0 collective-permute-done.3.refs_3_.refs_1_
  9.8 0.1 pack_fields.1
  9.8 3.0 %collective-permute-start.9 = (f32[2,128,128]{2,1,0:T(8,128)S(1)}, f32[2,128,128]{2,1,0:T(8,128)S(1)}, u32[]{:S(2)}, u32[]{:S(2)}) collective-permute-start(f32[2,128,128]{2,1,0:T(8,128)S(1)} %get-tuple-element.25), channel_id=1, source_target_pairs={{0,8},{4,12},{8,0},{12,4},{16,24},{20,28},{24,16},{28,20},{1,9},{5... | collective-permute-start | bytes 393224 | tf_op jit(solution)/shard_map/ppermute | solution.py:255
  12.8 1.5 %collective-permute-start.10 = (f32[2,128,128]{2,1,0:T(8,128)S(1)}, f32[2,128,128]{2,1,0:T(8,128)S(1)}, u32[]{:S(2)}, u32[]{:S(2)}) collective-permute-start(f32[2,128,128]{2,1,0:T(8,128)S(1)} %get-tuple-element.26), channel_id=1, source_target_pairs={{0,16},{4,20},{8,24},{12,28},{16,0},{20,4},{24,8},{28,12},{1,17},{... | collective-permute-start | bytes 393224 | tf_op jit(solution)/shard_map/ppermute | solution.py:255
  14.4 0.6 %collective-permute-start.11 = (f32[2,128,128]{2,1,0:T(8,128)S(1)}, f32[2,128,128]{2,1,0:T(8,128)S(1)}, u32[]{:S(2)}, u32[]{:S(2)}) collective-permute-start(f32[2,128,128]{2,1,0:T(8,128)S(1)} %get-tuple-element.27), channel_id=1, source_target_pairs={{0,24},{4,28},{8,16},{12,20},{16,8},{20,12},{24,0},{28,4},{1,25},{... | collective-permute-start | bytes 393224 | tf_op jit(solution)/shard_map/ppermute | solution.py:255
  14.9 0.0 collective-permute-done.1.below_ref
  14.9 0.0 collective-permute-done.above_ref
  14.9 0.0 copy-start
  15.0 3.4 %copy-done = f32[32,64,1024]{2,1,0:T(8,128)S(1)} copy-done((f32[32,64,1024]{2,1,0:T(8,128)S(1)}, f32[32,64,1024]{2,1,0:T(8,128)}, u32[]{:S(2)}) %copy-start) | copy-done | bytes 8388632
  18.3 6.9 %filter_slabs.1.slab_ref = f32[16,1152,128]{2,1,0:T(8,128)S(1)} custom-call(f32[32,64,1024]{2,1,0:T(8,128)S(1)} %copy-done, f32[32,1,1024]{2,1,0:T(1,128)S(1)} %collective-permute-done.above_ref, f32[32,1,1024]{2,1,0:T(1,128)S(1)} %collective-permute-done.1.below_ref), custom_call_target="tpu_custom_call" | custom-call | flops 16777216 | bytes 16777216 | tf_op jit(solution)/shard_map/filter_slabs/pallas_call | solution.py:81
  25.3 0.0 collective-permute-done.9.refs_2_
  25.3 0.0 collective-permute-done.10.refs_3_
  25.3 0.0 collective-permute-done.11.refs_4_
  25.3 2.2 %sum_lags.3 = (f32[2,256,128]{2,1,0:T(8,128)S(1)}, f32[2,256,128]{2,1,0:T(8,128)S(1)}) custom-call(f32[16,1152,128]{2,1,0:T(8,128)S(1)} %filter_slabs.1.slab_ref, f32[4,128,128]{2,1,0:T(8,128)S(1)} %get-tuple-element.18.refs_1_.refs_0_, f32[4,128,128]{2,1,0:T(8,128)S(1)} %collective-permute-done.3.refs_3_.refs_1_, ...), custom_call_target="tpu_custom_call" | custom-call | flops 16777216 | bytes 9437184 | tf_op jit(solution)/shard_map/sum_lags/pallas_call | solution.py:190
  27.5 1.6 %collective-permute-start.12 = (f32[2,256,128]{2,1,0:T(8,128)S(1)}, f32[2,256,128]{2,1,0:T(8,128)S(1)}, u32[]{:S(2)}, u32[]{:S(2)}) collective-permute-start(f32[2,256,128]{2,1,0:T(8,128)S(1)} %get-tuple-element.29), channel_id=1, source_target_pairs={{0,1},{1,0},{2,3},{3,2},{4,5},{5,4},{6,7},{7,6},{8,9},{9,8},{10,11... | collective-permute-start | bytes 786440 | tf_op jit(solution)/shard_map/ppermute | solution.py:279
  29.2 2.2 %collective-permute-start.4 = (f32[2,128,128]{2,1,0:T(8,128)S(1)}, f32[2,128,128]{2,1,0:T(8,128)S(1)}, u32[]{:S(2)}, u32[]{:S(2)}) collective-permute-start(f32[2,128,128]{2,1,0:T(8,128)S(1)} %get-tuple-element.20), channel_id=1, source_target_pairs={{0,8},{4,12},{8,0},{12,4},{16,24},{20,28},{24,16},{28,20},{1,9},{5... | collective-permute-start | bytes 393224 | tf_op jit(solution)/shard_map/ppermute | solution.py:255
  31.3 2.2 %collective-permute-start.5 = (f32[2,128,128]{2,1,0:T(8,128)S(1)}, f32[2,128,128]{2,1,0:T(8,128)S(1)}, u32[]{:S(2)}, u32[]{:S(2)}) collective-permute-start(f32[2,128,128]{2,1,0:T(8,128)S(1)} %get-tuple-element.21), channel_id=1, source_target_pairs={{0,16},{4,20},{8,24},{12,28},{16,0},{20,4},{24,8},{28,12},{1,17},{... | collective-permute-start | bytes 393224 | tf_op jit(solution)/shard_map/ppermute | solution.py:255
  33.5 1.5 %collective-permute-start.6 = (f32[2,128,128]{2,1,0:T(8,128)S(1)}, f32[2,128,128]{2,1,0:T(8,128)S(1)}, u32[]{:S(2)}, u32[]{:S(2)}) collective-permute-start(f32[2,128,128]{2,1,0:T(8,128)S(1)} %get-tuple-element.22), channel_id=1, source_target_pairs={{0,24},{4,28},{8,16},{12,20},{16,8},{20,12},{24,0},{28,4},{1,25},{... | collective-permute-start | bytes 393224 | tf_op jit(solution)/shard_map/ppermute | solution.py:255
  35.0 0.6 collective-permute-done.4.refs_2_
  35.6 4.0 %collective-permute-done.5.refs_3_ = f32[2,128,128]{2,1,0:T(8,128)S(1)} collective-permute-done((f32[2,128,128]{2,1,0:T(8,128)S(1)}, f32[2,128,128]{2,1,0:T(8,128)S(1)}, u32[]{:S(2)}, u32[]{:S(2)}) %collective-permute-start.5) | collective-permute-done | bytes 131104 | tf_op jit(solution)/shard_map/ppermute | solution.py:255
  39.6 0.0 collective-permute-done.6.refs_4_
  39.6 1.9 %sum_lags.2 = (f32[2,256,128]{2,1,0:T(8,128)S(1)}, f32[2,256,128]{2,1,0:T(8,128)S(1)}) custom-call(f32[16,1152,128]{2,1,0:T(8,128)S(1)} %filter_slabs.1.slab_ref, f32[4,128,128]{2,1,0:T(8,128)S(1)} %get-tuple-element.16.refs_0_, f32[4,128,128]{2,1,0:T(8,128)S(1)} %collective-permute-done.2.refs_2_.refs_1_, ...), custom_call_target="tpu_custom_call" | custom-call | flops 16777216 | bytes 9437184 | tf_op jit(solution)/shard_map/sum_lags/pallas_call | solution.py:190
  41.4 0.5 collective-permute-start.7
  42.0 0.0 collective-permute-done.12
  42.1 3.6 %collective-permute-start.13 = (f32[256,128]{1,0:T(8,128)S(1)}, f32[256,128]{1,0:T(8,128)S(1)}, u32[]{:S(2)}, u32[]{:S(2)}) collective-permute-start(f32[256,128]{1,0:T(8,128)S(1)} %get-tuple-element.32), channel_id=1, source_target_pairs={{0,3},{1,2},{2,1},{3,0},{4,7},{5,6},{6,5},{7,4},{8,11},{9,10},{10,... | collective-permute-start | bytes 393224 | tf_op jit(solution)/shard_map/ppermute | solution.py:279
  45.7 3.9 %collective-permute-done.7 = f32[2,256,128]{2,1,0:T(8,128)S(1)} collective-permute-done((f32[2,256,128]{2,1,0:T(8,128)S(1)}, f32[2,256,128]{2,1,0:T(8,128)S(1)}, u32[]{:S(2)}, u32[]{:S(2)}) %collective-permute-start.7) | collective-permute-done | bytes 262176 | tf_op jit(solution)/shard_map/ppermute | solution.py:279
  49.6 5.0 %collective-permute-start.8 = (f32[256,128]{1,0:T(8,128)S(1)}, f32[256,128]{1,0:T(8,128)S(1)}, u32[]{:S(2)}, u32[]{:S(2)}) collective-permute-start(f32[256,128]{1,0:T(8,128)S(1)} %get-tuple-element.34), channel_id=1, source_target_pairs={{0,3},{1,2},{2,1},{3,0},{4,7},{5,6},{6,5},{7,4},{8,11},{9,10},{10,... | collective-permute-start | bytes 393224 | tf_op jit(solution)/shard_map/ppermute | solution.py:279
  54.7 0.0 collective-permute-done.13.second_ref
  54.7 0.8 %turn_back.3 = f32[2,64,256]{2,1,0:T(8,128)} custom-call(f32[256,128]{1,0:T(8,128)S(1)} %get-tuple-element.33.first_ref, f32[256,128]{1,0:T(8,128)S(1)} %collective-permute-done.13.second_ref), custom_call_target="tpu_custom_call" | custom-call | tf_op jit(solution)/shard_map/turn_back/pallas_call | solution.py:294
  55.4 2.2 %collective-permute-done.8.second_ref = f32[256,128]{1,0:T(8,128)S(1)} collective-permute-done((f32[256,128]{1,0:T(8,128)S(1)}, f32[256,128]{1,0:T(8,128)S(1)}, u32[]{:S(2)}, u32[]{:S(2)}) %collective-permute-start.8) | collective-permute-done | bytes 131104 | tf_op jit(solution)/shard_map/ppermute | solution.py:279
  57.6 0.8 %turn_back.2 = f32[2,64,256]{2,1,0:T(8,128)} custom-call(f32[256,128]{1,0:T(8,128)S(1)} %get-tuple-element.35.first_ref, f32[256,128]{1,0:T(8,128)S(1)} %collective-permute-done.8.second_ref), custom_call_target="tpu_custom_call" | custom-call | tf_op jit(solution)/shard_map/turn_back/pallas_call | solution.py:294
  (4 shorter events, 0.1 us)
Async XLA Ops:
  0.6 1.0 %copy-start.1 = (f32[2,512,128]{2,1,0:T(8,128)S(1)}, f32[2,512,128]{2,1,0:T(8,128)}, u32[]{:S(2)}) copy-start(f32[2,512,128]{2,1,0:T(8,128)} %refs_0_.1) | copy-start | bytes 1572868
  1.7 1.0 %copy-start.2 = (f32[2,512,128]{2,1,0:T(8,128)S(1)}, f32[2,512,128]{2,1,0:T(8,128)}, u32[]{:S(2)}) copy-start(f32[2,512,128]{2,1,0:T(8,128)} %refs_1_.1) | copy-start | bytes 1572868
  3.1 6.7 %collective-permute-start.2 = (f32[4,128,128]{2,1,0:T(8,128)S(1)}, f32[4,128,128]{2,1,0:T(8,128)S(1)}, u32[]{:S(2)}, u32[]{:S(2)}) collective-permute-start(f32[4,128,128]{2,1,0:T(8,128)S(1)} %get-tuple-element.17), channel_id=1, source_target_pairs={{0,4},{4,0},{8,12},{12,8},{16,20},{20,16},{24,28},{28,24},{1,5},{5... | collective-permute-start | bytes 786440 | tf_op jit(solution)/shard_map/ppermute | solution.py:255
  3.6 6.2 %collective-permute-start.3 = (f32[4,128,128]{2,1,0:T(8,128)S(1)}, f32[4,128,128]{2,1,0:T(8,128)S(1)}, u32[]{:S(2)}, u32[]{:S(2)}) collective-permute-start(f32[4,128,128]{2,1,0:T(8,128)S(1)} %get-tuple-element.19), channel_id=1, source_target_pairs={{0,4},{4,0},{8,12},{12,8},{16,20},{20,16},{24,28},{28,24},{1,5},{5... | collective-permute-start | bytes 786440 | tf_op jit(solution)/shard_map/ppermute | solution.py:255
  5.4 9.5 %collective-permute-start.1 = (f32[32,1,1024]{2,1,0:T(1,128)S(1)}, f32[32,1,1024]{2,1,0:T(1,128)S(1)}, u32[]{:S(2)}, u32[]{:S(2)}) collective-permute-start(f32[32,1,1024]{2,1,0:T(1,128)S(1)} %get-tuple-element.30), channel_id=1, source_target_pairs={{4,0},{8,4},{12,8},{16,12},{20,16},{24,20},{28,24},{5,1},{9,5},{13... | collective-permute-start | bytes 393224 | tf_op jit(solution)/shard_map/ppermute | solution.py:24
  6.7 8.2 %collective-permute-start = (f32[32,1,1024]{2,1,0:T(1,128)S(1)}, f32[32,1,1024]{2,1,0:T(1,128)S(1)}, u32[]{:S(2)}, u32[]{:S(2)}) collective-permute-start(f32[32,1,1024]{2,1,0:T(1,128)S(1)} %get-tuple-element.31), channel_id=1, source_target_pairs={{0,4},{4,8},{8,12},{12,16},{16,20},{20,24},{24,28},{1,5},{5,9},{9,... | collective-permute-start | bytes 393224 | tf_op jit(solution)/shard_map/ppermute | solution.py:24
  9.8 15.4 %collective-permute-start.9 = (f32[2,128,128]{2,1,0:T(8,128)S(1)}, f32[2,128,128]{2,1,0:T(8,128)S(1)}, u32[]{:S(2)}, u32[]{:S(2)}) collective-permute-start(f32[2,128,128]{2,1,0:T(8,128)S(1)} %get-tuple-element.25), channel_id=1, source_target_pairs={{0,8},{4,12},{8,0},{12,4},{16,24},{20,28},{24,16},{28,20},{1,9},{5... | collective-permute-start | bytes 393224 | tf_op jit(solution)/shard_map/ppermute | solution.py:255
  12.8 12.5 %collective-permute-start.10 = (f32[2,128,128]{2,1,0:T(8,128)S(1)}, f32[2,128,128]{2,1,0:T(8,128)S(1)}, u32[]{:S(2)}, u32[]{:S(2)}) collective-permute-start(f32[2,128,128]{2,1,0:T(8,128)S(1)} %get-tuple-element.26), channel_id=1, source_target_pairs={{0,16},{4,20},{8,24},{12,28},{16,0},{20,4},{24,8},{28,12},{1,17},{... | collective-permute-start | bytes 393224 | tf_op jit(solution)/shard_map/ppermute | solution.py:255
  14.4 11.0 %collective-permute-start.11 = (f32[2,128,128]{2,1,0:T(8,128)S(1)}, f32[2,128,128]{2,1,0:T(8,128)S(1)}, u32[]{:S(2)}, u32[]{:S(2)}) collective-permute-start(f32[2,128,128]{2,1,0:T(8,128)S(1)} %get-tuple-element.27), channel_id=1, source_target_pairs={{0,24},{4,28},{8,16},{12,20},{16,8},{20,12},{24,0},{28,4},{1,25},{... | collective-permute-start | bytes 393224 | tf_op jit(solution)/shard_map/ppermute | solution.py:255
  14.9 3.4 %copy-start = (f32[32,64,1024]{2,1,0:T(8,128)S(1)}, f32[32,64,1024]{2,1,0:T(8,128)}, u32[]{:S(2)}) copy-start(f32[32,64,1024]{2,1,0:T(8,128)} %grad_hbm.1) | copy-start | bytes 25165828
  27.5 14.5 %collective-permute-start.12 = (f32[2,256,128]{2,1,0:T(8,128)S(1)}, f32[2,256,128]{2,1,0:T(8,128)S(1)}, u32[]{:S(2)}, u32[]{:S(2)}) collective-permute-start(f32[2,256,128]{2,1,0:T(8,128)S(1)} %get-tuple-element.29), channel_id=1, source_target_pairs={{0,1},{1,0},{2,3},{3,2},{4,5},{5,4},{6,7},{7,6},{8,9},{9,8},{10,11... | collective-permute-start | bytes 786440 | tf_op jit(solution)/shard_map/ppermute | solution.py:279
  29.2 6.4 %collective-permute-start.4 = (f32[2,128,128]{2,1,0:T(8,128)S(1)}, f32[2,128,128]{2,1,0:T(8,128)S(1)}, u32[]{:S(2)}, u32[]{:S(2)}) collective-permute-start(f32[2,128,128]{2,1,0:T(8,128)S(1)} %get-tuple-element.20), channel_id=1, source_target_pairs={{0,8},{4,12},{8,0},{12,4},{16,24},{20,28},{24,16},{28,20},{1,9},{5... | collective-permute-start | bytes 393224 | tf_op jit(solution)/shard_map/ppermute | solution.py:255
  31.3 8.2 %collective-permute-start.5 = (f32[2,128,128]{2,1,0:T(8,128)S(1)}, f32[2,128,128]{2,1,0:T(8,128)S(1)}, u32[]{:S(2)}, u32[]{:S(2)}) collective-permute-start(f32[2,128,128]{2,1,0:T(8,128)S(1)} %get-tuple-element.21), channel_id=1, source_target_pairs={{0,16},{4,20},{8,24},{12,28},{16,0},{20,4},{24,8},{28,12},{1,17},{... | collective-permute-start | bytes 393224 | tf_op jit(solution)/shard_map/ppermute | solution.py:255
  33.5 6.1 %collective-permute-start.6 = (f32[2,128,128]{2,1,0:T(8,128)S(1)}, f32[2,128,128]{2,1,0:T(8,128)S(1)}, u32[]{:S(2)}, u32[]{:S(2)}) collective-permute-start(f32[2,128,128]{2,1,0:T(8,128)S(1)} %get-tuple-element.22), channel_id=1, source_target_pairs={{0,24},{4,28},{8,16},{12,20},{16,8},{20,12},{24,0},{28,4},{1,25},{... | collective-permute-start | bytes 393224 | tf_op jit(solution)/shard_map/ppermute | solution.py:255
  41.4 8.1 %collective-permute-start.7 = (f32[2,256,128]{2,1,0:T(8,128)S(1)}, f32[2,256,128]{2,1,0:T(8,128)S(1)}, u32[]{:S(2)}, u32[]{:S(2)}) collective-permute-start(f32[2,256,128]{2,1,0:T(8,128)S(1)} %get-tuple-element.24), channel_id=1, source_target_pairs={{0,1},{1,0},{2,3},{3,2},{4,5},{5,4},{6,7},{7,6},{8,9},{9,8},{10,11... | collective-permute-start | bytes 786440 | tf_op jit(solution)/shard_map/ppermute | solution.py:279
  42.1 12.6 %collective-permute-start.13 = (f32[256,128]{1,0:T(8,128)S(1)}, f32[256,128]{1,0:T(8,128)S(1)}, u32[]{:S(2)}, u32[]{:S(2)}) collective-permute-start(f32[256,128]{1,0:T(8,128)S(1)} %get-tuple-element.32), channel_id=1, source_target_pairs={{0,3},{1,2},{2,1},{3,0},{4,7},{5,6},{6,5},{7,4},{8,11},{9,10},{10,... | collective-permute-start | bytes 393224 | tf_op jit(solution)/shard_map/ppermute | solution.py:279
  49.6 8.0 %collective-permute-start.8 = (f32[256,128]{1,0:T(8,128)S(1)}, f32[256,128]{1,0:T(8,128)S(1)}, u32[]{:S(2)}, u32[]{:S(2)}) collective-permute-start(f32[256,128]{1,0:T(8,128)S(1)} %get-tuple-element.34), channel_id=1, source_target_pairs={{0,3},{1,2},{2,1},{3,0},{4,7},{5,6},{6,5},{7,4},{8,11},{9,10},{10,... | collective-permute-start | bytes 393224 | tf_op jit(solution)/shard_map/ppermute | solution.py:279
where the time goes:
time: 58.7 us; the launch traced here: 58.4 us
  starting transfers between devices  26.7 us (45%)
  Pallas kernels  12.9 us (22%)
  waiting for transfers between devices  10.7 us (18%)
  local copies, waits for them, and re-layouts  7.25 us (12%)
  between operations  0.77 us (1%)
    ppermute x8, starting transfers between devices, swap(): lax.ppermute(part, 'strip', [(i, i ^ distance) for i in range(count)])  11.5 us
    ppermute x4, starting transfers between devices, exchange(): return lax.ppermute(parts, 'lag', [(i, i ^ distance) for i in range(count)])  10.8 us
    pallas_call x1, Pallas kernels, filter_slabs(): pl.pallas_call(functools.partial(filter_kernel, pad), out_shape=jax.Shape...  6.94 us
    ppermute x4, waiting for transfers between devices, exchange(): return lax.ppermute(parts, 'lag', [(i, i ^ distance) for i in range(count)])  6.06 us
    unnamed x6, local copies, waits for them, and re-layouts  5.46 us
    ppermute x8, waiting for transfers between devices, swap(): lax.ppermute(part, 'strip', [(i, i ^ distance) for i in range(count)])  4.62 us
    ppermute x2, starting transfers between devices, chain_halo(): return lax.ppermute(rows, axis, pairs)  4.33 us
    pallas_call x2, Pallas kernels, sum_lags(): pl.pallas_call(functools.partial(sum_kernel, sign, places, where_at), out...  4.08 us
  transfers between devices with their start and end apart: 14, of which 4 were waited for; matrix products, arithmetic and copies ran while one was open for 3% of the time, Pallas kernels for 16%

commit v1 on v0

--- a/solution.py
+++ b/solution.py
@@ -11,24 +11,33 @@
 ROWS = 8
 CLASSES = 4
 PAIRS = 4
+GROUPS = ((0,), (1,))
+FILTER_COST = 10**9
+FIRST_COST = 0
+SECOND_COST = 10**9
 FILTER_BYTES = 24 * 1024 * 1024
 SUM_BYTES = 8 * 1024 * 1024
 SMALL_BYTES = 4 * 1024 * 1024
 
+def weight(size):
+    return pl.CostEstimate(flops=size, bytes_accessed=size, transcendentals=0)
+
+
+def in_hbm(array):
+    return pltpu.with_memory_space_constraint(array, pltpu.HBM)
+
+
 whole_vmem = pl.BlockSpec(memory_space=pltpu.VMEM)
 
 
-def chain_halo(rows, axis, step):
-    count = lax.axis_size(axis)
-    pairs = [(i, i + step) for i in range(count) if 0 <= i + step < count]
-    return lax.ppermute(rows, axis, pairs)
-
-
-def filter_kernel(pad, grad_hbm, above_ref, below_ref, out_ref, *turned):
+def filter_kernel(pad, grad_hbm, near_ref, next_ref, out_ref, edges, *turned):
     lag_count, depth, width = grad_hbm.shape
     half = lag_count // 2
     tiles = width // LANES
     centers, uprights = turned[:PAIRS], turned[PAIRS:]
+    core = lax.rem(lax.axis_index("strip"), 2)
+    edges[1 - core] = near_ref[pl.ds(0, lag_count * tiles)]
+    edges[core] = next_ref[...]
     out_ref[:, pl.ds(0, pad)] = jnp.zeros((half, pad, LANES), jnp.float32)
     out_ref[:, pl.ds(pad + width, pad)] = jnp.zeros((half, pad, LANES), jnp.float32)
     for center_t in centers:
@@ -45,8 +54,8 @@
             for slab, shift in ((low_ref, 0), (high_ref, half)):
                 lag = step * PAIRS + within + shift
                 mid = slab[within, :, lanes]
-                up = jnp.where(row == 0, above_ref[lag, :, lanes], pltpu.roll(mid, 1, 0))
-                down = jnp.where(row == depth - 1, below_ref[lag, :, lanes], pltpu.roll(mid, depth - 1, 0))
+                up = jnp.where(row == 0, edges[0, pl.ds(lag + t * lag_count, 1)], pltpu.roll(mid, 1, 0))
+                down = jnp.where(row == depth - 1, edges[1, pl.ds(lag + t * lag_count, 1)], pltpu.roll(mid, depth - 1, 0))
                 mids.append(mid)
                 stencils.append(2.0 * mid - 0.25 * (up + down))
             centers[within][pl.ds(ROWS + t * LANES, LANES)] = jnp.concatenate(mids, 0).T
@@ -76,21 +85,20 @@
     )(grad_hbm, grad_hbm)
 
 
-def filter_slabs(image_grad, above, below, pad):
+def filter_slabs(image_grad, from_near, from_next, pad):
     lag_count, depth, width = image_grad.shape
     return pl.pallas_call(
         functools.partial(filter_kernel, pad),
         out_shape=jax.ShapeDtypeStruct((lag_count // 2, width + 2 * pad, 2 * depth), jnp.float32),
         in_specs=[pl.BlockSpec(memory_space=pltpu.HBM), whole_vmem, whole_vmem],
         out_specs=whole_vmem,
-        scratch_shapes=[pltpu.VMEM((width + 2 * ROWS, LANES), jnp.float32)] * PAIRS
+        scratch_shapes=[pltpu.VMEM((2, *from_next.shape), jnp.float32)]
+        + [pltpu.VMEM((width + 2 * ROWS, LANES), jnp.float32)] * PAIRS
         + [pltpu.VMEM((width, LANES), jnp.float32)] * PAIRS,
         compiler_params=pltpu.CompilerParams(vmem_limit_bytes=FILTER_BYTES),
-        cost_estimate=pl.CostEstimate(
-            flops=8 * lag_count * depth * width, bytes_accessed=8 * lag_count * depth * width, transcendentals=0
-        ),
+        cost_estimate=weight(FILTER_COST),
         name="filter_slabs",
-    )(image_grad, above, below)
+    )(in_hbm(image_grad), from_near, from_next)
 
 
 def sum_kernel(sign, places, where_at, slab_ref, *refs):
@@ -100,11 +108,10 @@
     if where_at is None:
         field_ref[...] = pieces[0][...]
     else:
-        columns = pieces[0].shape[-2]
         strip = lax.axis_index("strip")
-        for index, block, distance in where_at:
-            rows = pl.multiple_of((strip ^ distance) * columns, columns)
-            field_ref[pl.ds(rows, columns)] = pieces[index][block]
+        for index, row, distance in where_at:
+            rows = pl.multiple_of((strip ^ distance) * LANES, LANES)
+            field_ref[pl.ds(rows, LANES)] = pieces[index][pl.ds(row, LANES)]
     pad = (slab_rows - width) // 2
     lag_count = 2 * half
     margin = 2 * pad + 2 * half
@@ -198,80 +205,127 @@
             pltpu.VMEM((2, width + half, LANES), jnp.float32),
         ],
         compiler_params=pltpu.CompilerParams(vmem_limit_bytes=SUM_BYTES),
-        cost_estimate=pl.CostEstimate(
-            flops=8 * half * width * LANES, bytes_accessed=4 * half * slab_rows * LANES, transcendentals=0
-        ),
+        cost_estimate=weight(FIRST_COST if sign > 0 else SECOND_COST),
         name="sum_lags",
     )(slabs, *pieces)
 
 
-def cut_kernel(*refs):
-    half = len(refs) // 3
+def send_kernel(pieces, grad_hbm, *refs):
+    lag_count, depth, width = grad_hbm.shape
+    tiles = width // LANES
+    number = (len(refs) - 4) // 3
+    fields, near_ref, next_ref = refs[:number], refs[number], refs[number + 1]
+    mine = refs[number + 2 : 2 * number + 2]
+    held, edges, sems = refs[2 * number + 2 : 3 * number + 2], refs[-2], refs[-1]
     strip = lax.axis_index("strip")
-    for index, field_ref in enumerate(refs[:half]):
-        near_ref, far_ref = refs[half + 2 * index : half + 2 * index + 2]
-        snaps = field_ref.shape[0]
-        count, _, lanes = near_ref.shape
-        depth = lanes // snaps
-        for at in range(count):
-            for out_ref, side in ((far_ref, 1), (near_ref, 0)):
+    core = lax.rem(strip, 2)
+    copies = []
+    for side in range(2):
+        rows = pl.ds(side * (depth - ROWS), ROWS)
+        copies.append(pltpu.make_async_copy(grad_hbm.at[:, rows], edges.at[side], sems.at[side]))
+    for f in range(number):
+        copies.append(pltpu.make_async_copy(fields[f], held[f], sems.at[2 + f]))
+    for copy in copies:
+        copy.start()
+
+    for f in range(number):
+        copies[2 + f].wait()
+        snaps = held[f].shape[0]
+        for at in range(pieces):
+            for side in range(2):
                 first = pl.multiple_of((strip ^ (2 * at + side)) * depth, depth)
-                rows = [field_ref[s, pl.ds(first, depth)] for s in range(snaps)]
-                out_ref[at] = jnp.concatenate(rows, 0).T
-
-
-def pack_kernel(fields, *refs):
-    near, far, out = refs[:fields], refs[fields : 2 * fields], refs[2 * fields :]
-    distances = len(out) // fields
-    for f in range(fields):
-        for at in range(distances):
-            out[f * distances + at][0] = near[f][at + 1]
-            out[f * distances + at][1] = far[f][at + 1]
-
-
-def fields_by_rows(fields):
+                rows = [held[f][s, pl.ds(first, depth)] for s in range(snaps)]
+                piece = jnp.concatenate(rows, 0).T
+                if side:
+                    start = lag_count * tiles + (f * pieces + at) * LANES
+                    near_ref[pl.ds(start, LANES)] = piece
+                else:
+                    mine[f][pl.ds(at * LANES, LANES)] = piece
+
+    copies[0].wait()
+    copies[1].wait()
+    low = core == 0
+    for t in range(tiles):
+        lanes = pl.ds(t * LANES, LANES)
+        top = edges[0, :, 0, lanes]
+        bottom = edges[1, :, ROWS - 1, lanes]
+        rows = pl.ds(t * lag_count, lag_count)
+        near_ref[rows] = jnp.where(low, bottom, top)
+        next_ref[rows] = jnp.where(low, top, bottom)
+
+
+def pack_kernel(pieces, edge_rows, groups, *refs):
+    number = sum(len(group) for group in groups)
+    mine, near_ref, out = refs[:number], refs[number], refs[number + 1 :]
+    for g, group in enumerate(groups):
+        for at in range(1, pieces):
+            out_ref = out[g * (pieces - 1) + at - 1]
+            for place, f in enumerate(group):
+                rows = pl.ds(at * LANES, LANES)
+                out_ref[pl.ds(2 * place * LANES, LANES)] = mine[f][rows]
+                far = pl.ds(edge_rows + (f * pieces + at) * LANES, LANES)
+                out_ref[pl.ds((2 * place + 1) * LANES, LANES)] = near_ref[far]
+
+
+def strip_swap(part, distance):
+    count = lax.axis_size("strip")
+    return lax.ppermute(part, "strip", [(i, i ^ distance) for i in range(count)])
+
+
+def gather_rows(image_grad, fields):
+    lag_count, depth, width = image_grad.shape
     count = lax.axis_size("strip")
     snaps, all_rows, columns = fields[0].shape
-    depth = all_rows // count
-    if columns != LANES or count & (count - 1) or count < 4:
+    direct = columns == LANES and count >= 4 and count & (count - 1) == 0
+    pieces = count // 2 if direct else 0
+    number = len(fields) if direct else 0
+    edge_rows = lag_count * (width // LANES)
+
+    def buffer(rows):
+        return jax.ShapeDtypeStruct((rows, LANES), jnp.float32)
+
+    near, following, *mine = pl.pallas_call(
+        functools.partial(send_kernel, pieces),
+        out_shape=[buffer(edge_rows + number * pieces * LANES), buffer(edge_rows)]
+        + [buffer(pieces * LANES)] * number,
+        in_specs=[pl.BlockSpec(memory_space=pltpu.HBM)] * (1 + number),
+        out_specs=[whole_vmem] * (2 + number),
+        scratch_shapes=[pltpu.VMEM(f.shape, jnp.float32) for f in fields[:number]]
+        + [pltpu.VMEM((2, lag_count, ROWS, width), jnp.float32), pltpu.SemaphoreType.DMA((2 + number,))],
+        compiler_params=pltpu.CompilerParams(vmem_limit_bytes=SUM_BYTES),
+        name="send_rows",
+    )(*(in_hbm(a) for a in (image_grad, *fields[:number])))
+    near = strip_swap(near, 1)
+    following = lax.ppermute(
+        following, "strip", [p for i in range(1, count - 1, 2) for p in ((i, i + 1), (i + 1, i))]
+    )
+    if not direct:
         whole = []
         for field in fields:
             cut = field.reshape(snaps, count, depth, columns).transpose(1, 3, 0, 2)
             cut = lax.all_to_all(cut.reshape(count, columns, snaps * depth), "strip", 0, 0, tiled=True)
             whole.append([cut.reshape(count * columns, snaps * depth)])
-        return whole, None
-    number = len(fields)
-    cut = jax.ShapeDtypeStruct((count // 2, columns, snaps * depth), jnp.float32)
-    parts = pl.pallas_call(
-        cut_kernel,
-        out_shape=[cut] * (2 * number),
-        in_specs=[whole_vmem] * number,
-        out_specs=[whole_vmem] * (2 * number),
-        compiler_params=pltpu.CompilerParams(vmem_limit_bytes=SMALL_BYTES),
-        name="cut_fields",
-    )(*fields)
-
-    def swap(part, distance):
-        return lax.ppermute(part, "strip", [(i, i ^ distance) for i in range(count)])
-
-    near, far = parts[0::2], [swap(part, 1) for part in parts[1::2]]
-    distances = count // 2 - 1
-    pair = jax.ShapeDtypeStruct((2, columns, snaps * depth), jnp.float32)
+        return near, following, whole, [None] * len(fields)
+
+    out_shape = [buffer(2 * len(group) * LANES) for group in GROUPS for at in range(1, pieces)]
     packed = pl.pallas_call(
-        functools.partial(pack_kernel, number),
-        out_shape=[pair] * (distances * number),
-        in_specs=[whole_vmem] * (2 * number),
-        out_specs=[whole_vmem] * (distances * number),
+        functools.partial(pack_kernel, pieces, edge_rows, GROUPS),
+        out_shape=out_shape,
+        in_specs=[whole_vmem] * (number + 1),
+        out_specs=[whole_vmem] * len(out_shape),
         compiler_params=pltpu.CompilerParams(vmem_limit_bytes=SMALL_BYTES),
         name="pack_fields",
-    )(*near, *far)
-    where_at = [(0, 0, 0), (1, 0, 1)]
-    where_at += [(2 + at, side, 2 * at + 2 + side) for at in range(distances) for side in range(2)]
-    whole = []
-    for f in range(number):
-        sent = [swap(packed[f * distances + at], 2 * at + 2) for at in range(distances)]
-        whole.append([near[f], far[f], *sent])
-    return whole, where_at
+    )(*mine, near)
+    whole, where_at = [None] * number, [None] * number
+    for g, group in enumerate(GROUPS):
+        sent = [strip_swap(packed[g * (pieces - 1) + at - 1], 2 * at) for at in range(1, pieces)]
+        for place, f in enumerate(group):
+            whole[f] = [mine[f], near, *sent]
+            where_at[f] = [(0, 0, 0), (1, edge_rows + f * pieces * LANES, 1)]
+            where_at[f] += [
+                (1 + at, (2 * place + side) * LANES, 2 * at + side) for at in range(1, pieces) for side in range(2)
+            ]
+    return near, following, whole, where_at
 
 
 def exchange(parts, distance):
@@ -305,12 +359,12 @@
     lag_count, depth, width = image_grad.shape
     snaps = source_field.shape[0]
     pad = lax.axis_size("lag") * lag_count // 2
-    (receiver, source), where_at = fields_by_rows([receiver_field, source_field])
-    above = chain_halo(image_grad[:, depth - 1 :], "strip", 1)
-    below = chain_halo(image_grad[:, :1], "strip", -1)
-    slabs = filter_slabs(image_grad, above, below, pad)
-    source_adjoint = sum_places(*sum_lags(1, slabs, receiver, where_at, width), snaps)
-    receiver_adjoint = sum_places(*sum_lags(-1, slabs, source, where_at, width), snaps)
+    near, following, (receiver, source), (at_first, at_second) = gather_rows(
+        image_grad, [receiver_field, source_field]
+    )
+    slabs = filter_slabs(image_grad, near, following, pad)
+    source_adjoint = sum_places(*sum_lags(1, slabs, receiver, at_first, width), snaps)
+    receiver_adjoint = sum_places(*sum_lags(-1, slabs, source, at_second, width), snaps)
     return source_adjoint, receiver_adjoint
 
 

time: 58.7 us -> 51.5 us (0.88)
  local copies, waits for them, and re-layouts: 7.25 us -> 0.04 us
  starting transfers between devices: 26.7 us -> 21.4 us
  Pallas kernels: 12.9 us -> 15.9 us
  waiting for transfers between devices: 10.7 us -> 13.2 us
    unnamed x6 -> x0, local copies, waits for them, and re-layouts: 5.46 us -> none
    ppermute x10 -> x8, starting transfers between devices: 15.8 us -> 12 us  [the longest x7 11.3 us: strip_swap(): lax.ppermute(part, 'strip', [(i, i ^ distance) for i in range(count)])]
    ppermute x10 -> x8, waiting for transfers between devices: 4.62 us -> 6.82 us  [the longest x7 6.81 us: strip_swap(): lax.ppermute(part, 'strip', [(i, i ^ distance) for i in range(count)])]
    pallas_call x2, Pallas kernels: 0.38 us -> 2.35 us  [the longest x1 2.3 us: gather_rows(): pl.pallas_call(functools.partial(send_kernel, pieces), out_shape=[buffer(...]
    slice x1 -> x0, local copies, waits for them, and re-layouts: 1.76 us -> none  [local(): below = chain_halo(image_grad[:, :1], 'strip', -1)]
    ppermute x4, starting transfers between devices: 10.8 us -> 9.45 us  [exchange(): return lax.ppermute(parts, 'lag', [(i, i ^ distance) for i in range(count)])]
    pallas_call x1, Pallas kernels: 6.94 us -> 7.91 us  [filter_slabs(): pl.pallas_call(functools.partial(filter_kernel, pad), out_shape=jax.Shape...]
  transfers between devices with their start and end apart: 14 -> 12, of which waited for: 4 -> 7; matrix products, arithmetic and copies ran while one was open for 3% -> 0% of each run, Pallas kernels for 16% -> 21%
where the time goes in v1:
time: 51.5 us; the launch traced here: 51.3 us
  starting transfers between devices  21.4 us (42%)
  Pallas kernels  15.9 us (31%)
  waiting for transfers between devices  13.2 us (26%)
  between operations  0.72 us (1%)
    ppermute x7, starting transfers between devices, strip_swap(): lax.ppermute(part, 'strip', [(i, i ^ distance) for i in range(count)])  11.3 us
    ppermute x4, starting transfers between devices, exchange(): return lax.ppermute(parts, 'lag', [(i, i ^ distance) for i in range(count)])  9.45 us
    pallas_call x1, Pallas kernels, filter_slabs(): pl.pallas_call(functools.partial(filter_kernel, pad), out_shape=jax.Shape...  7.91 us
    ppermute x7, waiting for transfers between devices, strip_swap(): lax.ppermute(part, 'strip', [(i, i ^ distance) for i in range(count)])  6.81 us
    ppermute x4, waiting for transfers between devices, exchange(): return lax.ppermute(parts, 'lag', [(i, i ^ distance) for i in range(count)])  6.38 us
    pallas_call x2, Pallas kernels, sum_lags(): pl.pallas_call(functools.partial(sum_kernel, sign, places, where_at), out...  4.07 us
    pallas_call x1, Pallas kernels, gather_rows(): pl.pallas_call(functools.partial(send_kernel, pieces), out_shape=[buffer(...  2.3 us
    pallas_call x2, Pallas kernels, sum_places(): pl.pallas_call(turn_back_kernel, out_shape=jax.ShapeDtypeStruct((snaps, l...  1.52 us
  transfers between devices with their start and end apart: 12, of which 7 were waited for; matrix products, arithmetic and copies ran while one was open for 0% of the time, Pallas kernels for 21%

profile of v1, /device:TPU:0, one launch (start us, length us, event | category | flops | bytes accessed | tf_op | source)
XLA Modules:
  0.0 51.3 jit_solution(10180151451597169429)
XLA Ops:
  0.6 2.3 %send_rows.1 = (f32[1280,128]{1,0:T(8,128)S(1)}, f32[256,128]{1,0:T(8,128)S(1)}, f32[512,128]{1,0:T(8,128)S(1)}, f32[512,128]{1,0:T(8,128)S(1)}) custom-call(f32[32,64,1024]{2,1,0:T(8,128)} %grad_hbm.3, f32[2,512,128]{2,1,0:T(8,128)} %refs_0_.1, f32[2,512,128]{2,1,0:T(8,128)} %refs_1_.1), custom_call_target="tpu_custom_call" | custom-call | tf_op jit(solution)/shard_map/send_rows/pallas_call | solution.py:287
  2.9 0.5 %collective-permute-start = (f32[1280,128]{1,0:T(8,128)S(1)}, f32[1280,128]{1,0:T(8,128)S(1)}, u32[]{:S(2)}, u32[]{:S(2)}) collective-permute-start(f32[1280,128]{1,0:T(8,128)S(1)} %get-tuple-element.16), channel_id=1, source_target_pairs={{0,4},{4,0},{8,12},{12,8},{16,20},{20,16},{24,28},{28,24},{1,5},{5... | collective-permute-start | bytes 1966088 | tf_op jit(solution)/shard_map/ppermute | solution.py:272
  3.5 0.7 %collective-permute-start.1 = (f32[256,128]{1,0:T(8,128)S(1)}, f32[256,128]{1,0:T(8,128)S(1)}, u32[]{:S(2)}, u32[]{:S(2)}) collective-permute-start(f32[256,128]{1,0:T(8,128)S(1)} %get-tuple-element.17), channel_id=1, source_target_pairs={{4,8},{8,4},{12,16},{16,12},{20,24},{24,20},{5,9},{9,5},{13,17},{1... | collective-permute-start | bytes 393224 | tf_op jit(solution)/shard_map/ppermute | solution.py:299
  4.1 1.1 %collective-permute-done.near_ref.refs_2_.refs_1_ = f32[1280,128]{1,0:T(8,128)S(1)} collective-permute-done((f32[1280,128]{1,0:T(8,128)S(1)}, f32[1280,128]{1,0:T(8,128)S(1)}, u32[]{:S(2)}, u32[]{:S(2)}) %collective-permute-start) | collective-permute-done | bytes 655392 | tf_op jit(solution)/shard_map/ppermute | solution.py:272
  5.2 0.1 pack_fields.1
  5.2 2.9 %collective-permute-start.7 = (f32[256,128]{1,0:T(8,128)S(1)}, f32[256,128]{1,0:T(8,128)S(1)}, u32[]{:S(2)}, u32[]{:S(2)}) collective-permute-start(f32[256,128]{1,0:T(8,128)S(1)} %get-tuple-element.25), channel_id=1, source_target_pairs={{0,8},{4,12},{8,0},{12,4},{16,24},{20,28},{24,16},{28,20},{1,9},{5... | collective-permute-start | bytes 393224 | tf_op jit(solution)/shard_map/ppermute | solution.py:272
  8.2 2.0 %collective-permute-start.8 = (f32[256,128]{1,0:T(8,128)S(1)}, f32[256,128]{1,0:T(8,128)S(1)}, u32[]{:S(2)}, u32[]{:S(2)}) collective-permute-start(f32[256,128]{1,0:T(8,128)S(1)} %get-tuple-element.26), channel_id=1, source_target_pairs={{0,16},{4,20},{8,24},{12,28},{16,0},{20,4},{24,8},{28,12},{1,17},{... | collective-permute-start | bytes 393224 | tf_op jit(solution)/shard_map/ppermute | solution.py:272
  10.2 0.9 %collective-permute-start.9 = (f32[256,128]{1,0:T(8,128)S(1)}, f32[256,128]{1,0:T(8,128)S(1)}, u32[]{:S(2)}, u32[]{:S(2)}) collective-permute-start(f32[256,128]{1,0:T(8,128)S(1)} %get-tuple-element.27), channel_id=1, source_target_pairs={{0,24},{4,28},{8,16},{12,20},{16,8},{20,12},{24,0},{28,4},{1,25},{... | collective-permute-start | bytes 393224 | tf_op jit(solution)/shard_map/ppermute | solution.py:272
  11.0 0.0 collective-permute-done.1.next_ref
  11.0 7.9 %filter_slabs.1.slab_ref = f32[16,1152,128]{2,1,0:T(8,128)S(1)} custom-call(f32[32,64,1024]{2,1,0:T(8,128)} %grad_hbm.3, f32[1280,128]{1,0:T(8,128)S(1)} %collective-permute-done.near_ref.refs_2_.refs_1_, f32[256,128]{1,0:T(8,128)S(1)} %collective-permute-done.1.next_ref), custom_call_target="tpu_custom_call" | custom-call | flops 1000000000 | bytes 1000000000 | tf_op jit(solution)/shard_map/filter_slabs/pallas_call | solution.py:90
  18.9 0.0 collective-permute-done.7.refs_2_
  19.0 0.0 collective-permute-done.8.refs_3_
  19.0 0.0 collective-permute-done.9.refs_4_
  19.0 2.2 %sum_lags.3 = (f32[2,256,128]{2,1,0:T(8,128)S(1)}, f32[2,256,128]{2,1,0:T(8,128)S(1)}) custom-call(f32[16,1152,128]{2,1,0:T(8,128)S(1)} %filter_slabs.1.slab_ref, f32[512,128]{1,0:T(8,128)S(1)} %get-tuple-element.19.refs_1_.refs_0_, f32[1280,128]{1,0:T(8,128)S(1)} %collective-permute-done.near_ref.refs_2_.refs_1_, ...), custom_call_target="tpu_custom_call" | custom-call | flops 1000000000 | bytes 1000000000 | tf_op jit(solution)/shard_map/sum_lags/pallas_call | solution.py:197
  21.2 1.6 %collective-permute-start.10 = (f32[2,256,128]{2,1,0:T(8,128)S(1)}, f32[2,256,128]{2,1,0:T(8,128)S(1)}, u32[]{:S(2)}, u32[]{:S(2)}) collective-permute-start(f32[2,256,128]{2,1,0:T(8,128)S(1)} %get-tuple-element.29), channel_id=1, source_target_pairs={{0,1},{1,0},{2,3},{3,2},{4,5},{5,4},{6,7},{7,6},{8,9},{9,8},{10,11... | collective-permute-start | bytes 786440 | tf_op jit(solution)/shard_map/ppermute | solution.py:333
  22.9 1.2 %collective-permute-start.2 = (f32[256,128]{1,0:T(8,128)S(1)}, f32[256,128]{1,0:T(8,128)S(1)}, u32[]{:S(2)}, u32[]{:S(2)}) collective-permute-start(f32[256,128]{1,0:T(8,128)S(1)} %get-tuple-element.20), channel_id=1, source_target_pairs={{0,8},{4,12},{8,0},{12,4},{16,24},{20,28},{24,16},{28,20},{1,9},{5... | collective-permute-start | bytes 393224 | tf_op jit(solution)/shard_map/ppermute | solution.py:272
  24.1 2.3 %collective-permute-start.3 = (f32[256,128]{1,0:T(8,128)S(1)}, f32[256,128]{1,0:T(8,128)S(1)}, u32[]{:S(2)}, u32[]{:S(2)}) collective-permute-start(f32[256,128]{1,0:T(8,128)S(1)} %get-tuple-element.21), channel_id=1, source_target_pairs={{0,16},{4,20},{8,24},{12,28},{16,0},{20,4},{24,8},{28,12},{1,17},{... | collective-permute-start | bytes 393224 | tf_op jit(solution)/shard_map/ppermute | solution.py:272
  26.4 1.4 %collective-permute-start.4 = (f32[256,128]{1,0:T(8,128)S(1)}, f32[256,128]{1,0:T(8,128)S(1)}, u32[]{:S(2)}, u32[]{:S(2)}) collective-permute-start(f32[256,128]{1,0:T(8,128)S(1)} %get-tuple-element.22), channel_id=1, source_target_pairs={{0,24},{4,28},{8,16},{12,20},{16,8},{20,12},{24,0},{28,4},{1,25},{... | collective-permute-start | bytes 393224 | tf_op jit(solution)/shard_map/ppermute | solution.py:272
  27.9 0.4 collective-permute-done.2.refs_2_
  28.3 4.0 %collective-permute-done.3.refs_3_ = f32[256,128]{1,0:T(8,128)S(1)} collective-permute-done((f32[256,128]{1,0:T(8,128)S(1)}, f32[256,128]{1,0:T(8,128)S(1)}, u32[]{:S(2)}, u32[]{:S(2)}) %collective-permute-start.3) | collective-permute-done | bytes 131104 | tf_op jit(solution)/shard_map/ppermute | solution.py:272
  32.3 1.3 %collective-permute-done.4.refs_4_ = f32[256,128]{1,0:T(8,128)S(1)} collective-permute-done((f32[256,128]{1,0:T(8,128)S(1)}, f32[256,128]{1,0:T(8,128)S(1)}, u32[]{:S(2)}, u32[]{:S(2)}) %collective-permute-start.4) | collective-permute-done | bytes 131104 | tf_op jit(solution)/shard_map/ppermute | solution.py:272
  33.6 1.9 %sum_lags.2 = (f32[2,256,128]{2,1,0:T(8,128)S(1)}, f32[2,256,128]{2,1,0:T(8,128)S(1)}) custom-call(f32[16,1152,128]{2,1,0:T(8,128)S(1)} %filter_slabs.1.slab_ref, f32[512,128]{1,0:T(8,128)S(1)} %get-tuple-element.18.refs_0_, f32[1280,128]{1,0:T(8,128)S(1)} %collective-permute-done.near_ref.refs_2_.refs_1_, f32[256,128]{1,0:T(8,128)S(1)} %collective-permute-done.2.refs_2_, ...), custom_call_target="tpu_custom_call" | custom-call | tf_op jit(solution)/shard_map/sum_lags/pallas_call | solution.py:197
  35.5 0.5 %collective-permute-start.5 = (f32[2,256,128]{2,1,0:T(8,128)S(1)}, f32[2,256,128]{2,1,0:T(8,128)S(1)}, u32[]{:S(2)}, u32[]{:S(2)}) collective-permute-start(f32[2,256,128]{2,1,0:T(8,128)S(1)} %get-tuple-element.24), channel_id=1, source_target_pairs={{0,1},{1,0},{2,3},{3,2},{4,5},{5,4},{6,7},{7,6},{8,9},{9,8},{10,11... | collective-permute-start | bytes 786440 | tf_op jit(solution)/shard_map/ppermute | solution.py:333
  36.0 0.0 collective-permute-done.10
  36.1 3.6 %collective-permute-start.11 = (f32[256,128]{1,0:T(8,128)S(1)}, f32[256,128]{1,0:T(8,128)S(1)}, u32[]{:S(2)}, u32[]{:S(2)}) collective-permute-start(f32[256,128]{1,0:T(8,128)S(1)} %get-tuple-element.30), channel_id=1, source_target_pairs={{0,3},{1,2},{2,1},{3,0},{4,7},{5,6},{6,5},{7,4},{8,11},{9,10},{10,... | collective-permute-start | bytes 393224 | tf_op jit(solution)/shard_map/ppermute | solution.py:333
  39.7 3.1 %collective-permute-done.5 = f32[2,256,128]{2,1,0:T(8,128)S(1)} collective-permute-done((f32[2,256,128]{2,1,0:T(8,128)S(1)}, f32[2,256,128]{2,1,0:T(8,128)S(1)}, u32[]{:S(2)}, u32[]{:S(2)}) %collective-permute-start.5) | collective-permute-done | bytes 262176 | tf_op jit(solution)/shard_map/ppermute | solution.py:333
  42.8 3.6 %collective-permute-start.6 = (f32[256,128]{1,0:T(8,128)S(1)}, f32[256,128]{1,0:T(8,128)S(1)}, u32[]{:S(2)}, u32[]{:S(2)}) collective-permute-start(f32[256,128]{1,0:T(8,128)S(1)} %get-tuple-element.32), channel_id=1, source_target_pairs={{0,3},{1,2},{2,1},{3,0},{4,7},{5,6},{6,5},{7,4},{8,11},{9,10},{10,... | collective-permute-start | bytes 393224 | tf_op jit(solution)/shard_map/ppermute | solution.py:333
  46.5 2.7 %collective-permute-done.11.second_ref = f32[256,128]{1,0:T(8,128)S(1)} collective-permute-done((f32[256,128]{1,0:T(8,128)S(1)}, f32[256,128]{1,0:T(8,128)S(1)}, u32[]{:S(2)}, u32[]{:S(2)}) %collective-permute-start.11) | collective-permute-done | bytes 131104 | tf_op jit(solution)/shard_map/ppermute | solution.py:333
  49.1 0.8 %turn_back.3 = f32[2,64,256]{2,1,0:T(8,128)} custom-call(f32[256,128]{1,0:T(8,128)S(1)} %get-tuple-element.31.first_ref, f32[256,128]{1,0:T(8,128)S(1)} %collective-permute-done.11.second_ref), custom_call_target="tpu_custom_call" | custom-call | tf_op jit(solution)/shard_map/turn_back/pallas_call | solution.py:348
  49.9 0.7 %collective-permute-done.6.second_ref = f32[256,128]{1,0:T(8,128)S(1)} collective-permute-done((f32[256,128]{1,0:T(8,128)S(1)}, f32[256,128]{1,0:T(8,128)S(1)}, u32[]{:S(2)}, u32[]{:S(2)}) %collective-permute-start.6) | collective-permute-done | bytes 131104 | tf_op jit(solution)/shard_map/ppermute | solution.py:333
  50.5 0.8 %turn_back.2 = f32[2,64,256]{2,1,0:T(8,128)} custom-call(f32[256,128]{1,0:T(8,128)S(1)} %get-tuple-element.33.first_ref, f32[256,128]{1,0:T(8,128)S(1)} %collective-permute-done.6.second_ref), custom_call_target="tpu_custom_call" | custom-call | tf_op jit(solution)/shard_map/turn_back/pallas_call | solution.py:348
  (4 shorter events, 0.1 us)
Async XLA Ops:
  2.9 2.2 %collective-permute-start = (f32[1280,128]{1,0:T(8,128)S(1)}, f32[1280,128]{1,0:T(8,128)S(1)}, u32[]{:S(2)}, u32[]{:S(2)}) collective-permute-start(f32[1280,128]{1,0:T(8,128)S(1)} %get-tuple-element.16), channel_id=1, source_target_pairs={{0,4},{4,0},{8,12},{12,8},{16,20},{20,16},{24,28},{28,24},{1,5},{5... | collective-permute-start | bytes 1966088 | tf_op jit(solution)/shard_map/ppermute | solution.py:272
  3.5 7.6 %collective-permute-start.1 = (f32[256,128]{1,0:T(8,128)S(1)}, f32[256,128]{1,0:T(8,128)S(1)}, u32[]{:S(2)}, u32[]{:S(2)}) collective-permute-start(f32[256,128]{1,0:T(8,128)S(1)} %get-tuple-element.17), channel_id=1, source_target_pairs={{4,8},{8,4},{12,16},{16,12},{20,24},{24,20},{5,9},{9,5},{13,17},{1... | collective-permute-start | bytes 393224 | tf_op jit(solution)/shard_map/ppermute | solution.py:299
  5.2 13.7 %collective-permute-start.7 = (f32[256,128]{1,0:T(8,128)S(1)}, f32[256,128]{1,0:T(8,128)S(1)}, u32[]{:S(2)}, u32[]{:S(2)}) collective-permute-start(f32[256,128]{1,0:T(8,128)S(1)} %get-tuple-element.25), channel_id=1, source_target_pairs={{0,8},{4,12},{8,0},{12,4},{16,24},{20,28},{24,16},{28,20},{1,9},{5... | collective-permute-start | bytes 393224 | tf_op jit(solution)/shard_map/ppermute | solution.py:272
  8.2 10.8 %collective-permute-start.8 = (f32[256,128]{1,0:T(8,128)S(1)}, f32[256,128]{1,0:T(8,128)S(1)}, u32[]{:S(2)}, u32[]{:S(2)}) collective-permute-start(f32[256,128]{1,0:T(8,128)S(1)} %get-tuple-element.26), channel_id=1, source_target_pairs={{0,16},{4,20},{8,24},{12,28},{16,0},{20,4},{24,8},{28,12},{1,17},{... | collective-permute-start | bytes 393224 | tf_op jit(solution)/shard_map/ppermute | solution.py:272
  10.2 8.8 %collective-permute-start.9 = (f32[256,128]{1,0:T(8,128)S(1)}, f32[256,128]{1,0:T(8,128)S(1)}, u32[]{:S(2)}, u32[]{:S(2)}) collective-permute-start(f32[256,128]{1,0:T(8,128)S(1)} %get-tuple-element.27), channel_id=1, source_target_pairs={{0,24},{4,28},{8,16},{12,20},{16,8},{20,12},{24,0},{28,4},{1,25},{... | collective-permute-start | bytes 393224 | tf_op jit(solution)/shard_map/ppermute | solution.py:272
  21.2 14.8 %collective-permute-start.10 = (f32[2,256,128]{2,1,0:T(8,128)S(1)}, f32[2,256,128]{2,1,0:T(8,128)S(1)}, u32[]{:S(2)}, u32[]{:S(2)}) collective-permute-start(f32[2,256,128]{2,1,0:T(8,128)S(1)} %get-tuple-element.29), channel_id=1, source_target_pairs={{0,1},{1,0},{2,3},{3,2},{4,5},{5,4},{6,7},{7,6},{8,9},{9,8},{10,11... | collective-permute-start | bytes 786440 | tf_op jit(solution)/shard_map/ppermute | solution.py:333
  22.9 5.4 %collective-permute-start.2 = (f32[256,128]{1,0:T(8,128)S(1)}, f32[256,128]{1,0:T(8,128)S(1)}, u32[]{:S(2)}, u32[]{:S(2)}) collective-permute-start(f32[256,128]{1,0:T(8,128)S(1)} %get-tuple-element.20), channel_id=1, source_target_pairs={{0,8},{4,12},{8,0},{12,4},{16,24},{20,28},{24,16},{28,20},{1,9},{5... | collective-permute-start | bytes 393224 | tf_op jit(solution)/shard_map/ppermute | solution.py:272
  24.1 8.2 %collective-permute-start.3 = (f32[256,128]{1,0:T(8,128)S(1)}, f32[256,128]{1,0:T(8,128)S(1)}, u32[]{:S(2)}, u32[]{:S(2)}) collective-permute-start(f32[256,128]{1,0:T(8,128)S(1)} %get-tuple-element.21), channel_id=1, source_target_pairs={{0,16},{4,20},{8,24},{12,28},{16,0},{20,4},{24,8},{28,12},{1,17},{... | collective-permute-start | bytes 393224 | tf_op jit(solution)/shard_map/ppermute | solution.py:272
  26.4 7.2 %collective-permute-start.4 = (f32[256,128]{1,0:T(8,128)S(1)}, f32[256,128]{1,0:T(8,128)S(1)}, u32[]{:S(2)}, u32[]{:S(2)}) collective-permute-start(f32[256,128]{1,0:T(8,128)S(1)} %get-tuple-element.22), channel_id=1, source_target_pairs={{0,24},{4,28},{8,16},{12,20},{16,8},{20,12},{24,0},{28,4},{1,25},{... | collective-permute-start | bytes 393224 | tf_op jit(solution)/shard_map/ppermute | solution.py:272
  35.5 7.3 %collective-permute-start.5 = (f32[2,256,128]{2,1,0:T(8,128)S(1)}, f32[2,256,128]{2,1,0:T(8,128)S(1)}, u32[]{:S(2)}, u32[]{:S(2)}) collective-permute-start(f32[2,256,128]{2,1,0:T(8,128)S(1)} %get-tuple-element.24), channel_id=1, source_target_pairs={{0,1},{1,0},{2,3},{3,2},{4,5},{5,4},{6,7},{7,6},{8,9},{9,8},{10,11... | collective-permute-start | bytes 786440 | tf_op jit(solution)/shard_map/ppermute | solution.py:333
  36.1 13.0 %collective-permute-start.11 = (f32[256,128]{1,0:T(8,128)S(1)}, f32[256,128]{1,0:T(8,128)S(1)}, u32[]{:S(2)}, u32[]{:S(2)}) collective-permute-start(f32[256,128]{1,0:T(8,128)S(1)} %get-tuple-element.30), channel_id=1, source_target_pairs={{0,3},{1,2},{2,1},{3,0},{4,7},{5,6},{6,5},{7,4},{8,11},{9,10},{10,... | collective-permute-start | bytes 393224 | tf_op jit(solution)/shard_map/ppermute | solution.py:333
  42.8 7.7 %collective-permute-start.6 = (f32[256,128]{1,0:T(8,128)S(1)}, f32[256,128]{1,0:T(8,128)S(1)}, u32[]{:S(2)}, u32[]{:S(2)}) collective-permute-start(f32[256,128]{1,0:T(8,128)S(1)} %get-tuple-element.32), channel_id=1, source_target_pairs={{0,3},{1,2},{2,1},{3,0},{4,7},{5,6},{6,5},{7,4},{8,11},{9,10},{10,... | collective-permute-start | bytes 393224 | tf_op jit(solution)/shard_map/ppermute | solution.py:333
